TPU v7x, 1024 devices: a whole 4x4x32 slice. The times are simulated.
1024 devices in a mesh: outer: 64 (over z, y_lo), blk: 16 (over y_hi, x, core).
Axes of the slice: x: 4, y: 4 (y_hi: 2, y_lo: 2; y = y_hi * 2 + y_lo), z: 32, core: 2. Of those that a mesh axis runs over, the one named last changes fastest.
Arguments:
- picture_embeds: bfloat16 [262144, 1152], P(('outer', 'blk')), may hold values from -0.1875 to 0.1875
- caption_embeds: bfloat16 [262144, 1152], P(('outer', 'blk')), may hold values from -0.1875 to 0.1875
- sharpness_factor: float32 [1], replicated, may hold values from 60 to 120
- offset_term: float32 [1], replicated, may hold values from -4 to -2
Outputs:
- image_grad: float32 [262144, 1152], P(('outer', 'blk'))
- caption_derivative: float32 [262144, 1152], P(('outer', 'blk'))
All inputs are finite; a program needn't handle non-finite values.
Results may differ from a plain program's by a relative error of at most 0.007.
Values may be sent and summed in bfloat16 or wider, within the bound.
No kernel may reach another device: no remote copies, remote signals or barrier semaphores. Data moves between devices by JAX's collectives and lax.ppermute only.
A program may use at most 32 MiB of HBM per device.

v0:
```python
import jax
import jax.numpy as jnp
from jax import lax
from jax.experimental import pallas as pl
from jax.experimental.pallas import tpu as pltpu
from jax.sharding import PartitionSpec as P

HALF = 2
SPAN = 2 * HALF + 1
AXES = ("outer", "blk")
MIB = 1024 * 1024
CHUNKS = 4
F32, BF16 = jnp.float32, jnp.bfloat16


def inverse_norm(wide):
    return 1.0 / jnp.sqrt(jnp.sum(wide * wide, axis=-1, keepdims=True) + 1e-06)


def normalized(block):
    wide = block.astype(F32)
    return (wide * inverse_norm(wide)).astype(BF16)


def dot(a, b):
    return jnp.dot(a, b, preferred_element_type=F32)


def logits(scale, offset, own_n, other_n):
    z = lax.dot_general(own_n, other_n, (((1,), (1,)), ((), ())), preferred_element_type=F32)
    return scale[0] * z + offset[0]


def pair_grad(scale, offset, own_n, other_n):
    return (jax.nn.sigmoid(logits(scale, offset, own_n, other_n)) / SPAN).astype(BF16)


def halves(ref):
    rows = ref.shape[0] // 2
    return ref[:rows], ref[rows:]


def side_grads(scale, offset, mine, theirs):
    return [pair_grad(scale, offset, own_n, other_n) for own_n, other_n in zip(mine, theirs[::-1])]


def prepare_kernel(x, y, pair, raw, sem):
    rows = x.shape[0]
    step = rows // CHUNKS
    copies = []
    for side, source in enumerate((x, y)):
        for c in range(CHUNKS):
            copies.append(
                pltpu.make_async_copy(
                    source.at[pl.ds(c * step, step)],
                    raw.at[pl.ds(side * rows + c * step, step)],
                    sem.at[side * CHUNKS + c],
                )
            )
    for copy in copies:
        copy.start()
    for c, copy in enumerate(copies):
        copy.wait()
        part = slice(c * step, (c + 1) * step)
        wide = raw[part].astype(F32)
        pair[part] = (wide * inverse_norm(wide)).astype(BF16)


def early_kernel(rim, scale, offset, pair, mate_x, mate_y, picked, mates, own_grad, mate_grad_x, mate_grad_y):
    rows = mate_x.shape[0]
    mates[:rows] = normalized(mate_x[...])
    mates[rows:] = normalized(mate_y[...])

    @pl.when(rim[0] == 1)
    def _():
        picked[...] = mates[...]

    @pl.when(rim[0] != 1)
    def _():
        picked[...] = pair[...]

    mine = halves(pair)
    z = logits(scale, offset, *mine)
    rows = lax.broadcasted_iota(jnp.int32, z.shape, 0)
    cols = lax.broadcasted_iota(jnp.int32, z.shape, 1)
    label = jnp.where(rows == cols, 1.0, -1.0).astype(F32)
    own_grad[...] = (-label * jax.nn.sigmoid(-label * z) / SPAN).astype(BF16)
    mate_grad_x[...], mate_grad_y[...] = side_grads(scale, offset, mine, halves(mates))


def middle_kernel(
    scale, offset, pair, mates, own_grad, mate_grad_x, mate_grad_y, near, sum_x, sum_y, held, sem
):
    copy = pltpu.make_async_copy(near, held, sem)
    copy.start()
    mine = halves(pair)
    mate_x, mate_y = halves(mates)
    sum_x[...] = dot(own_grad[...], mine[1]) + dot(mate_grad_x[...], mate_y)
    sum_y[...] = lax.dot_general(
        own_grad[...], mine[0], (((0,), (0,)), ((), ())), preferred_element_type=F32
    ) + dot(mate_grad_y[...], mate_x)
    copy.wait()
    nears = halves(held)
    grad_x, grad_y = side_grads(scale, offset, mine, nears)
    sum_x[...] += dot(grad_x, nears[1])
    sum_y[...] += dot(grad_y, nears[0])


def end_kernel(
    rim, scale, offset, pair, total_x, total_y, far, relayed, x, y, late,
    out_x, out_y, full, raw, spare, raw_sem, spare_sem, sem,
):
    rows = total_x.shape[0]
    step = rows // CHUNKS
    loads = [
        pltpu.make_async_copy(source, raw.at[pl.ds(side * rows, rows)], raw_sem.at[side])
        for side, source in enumerate((x, y))
    ]
    for load in loads:
        load.start()
    mine, fars = halves(pair), halves(far)
    relays = halves(relayed)
    far_grads = side_grads(scale, offset, mine, fars)
    relay_grads = side_grads(scale, offset, mine, relays)
    for side, total in enumerate((total_x, total_y)):
        full[side * rows : (side + 1) * rows] = (
            total[...] + dot(far_grads[side], fars[1 - side]) + dot(relay_grads[side], relays[1 - side])
        )

    @pl.when(rim[0] > 0)
    def _():
        copy = pltpu.make_async_copy(late, spare, spare_sem)
        copy.start()
        copy.wait()
        lates = halves(spare)
        late_grads = side_grads(scale, offset, mine, lates)
        for side in range(2):
            full[side * rows : (side + 1) * rows] += dot(late_grads[side], lates[1 - side])

    copies = []
    for side, out in enumerate((out_x, out_y)):
        loads[side].wait()
        for c in range(CHUNKS):
            part = slice(side * rows + c * step, side * rows + (c + 1) * step)
            wide = raw[part].astype(F32)
            inv = inverse_norm(wide)
            grad = scale[0] * full[part]
            along = inv * inv * jnp.sum(wide * grad, axis=-1, keepdims=True)
            full[part] = (grad - wide * along) * inv
            copy = pltpu.make_async_copy(
                full.at[pl.ds(side * rows + c * step, step)],
                out.at[pl.ds(c * step, step)],
                sem.at[side * CHUNKS + c],
            )
            copy.start()
            copies.append(copy)
    for copy in copies:
        copy.wait()


VMEM = pl.BlockSpec(memory_space=pltpu.VMEM)
SMEM = pl.BlockSpec(memory_space=pltpu.SMEM)
ANY = pl.BlockSpec(memory_space=pl.ANY)


def call(kernel, outs, arrays, small=0, loose=0, in_spec=VMEM, out_spec=VMEM, scratch=()):
    return pl.pallas_call(
        kernel,
        out_shape=[jax.ShapeDtypeStruct(*o) for o in outs],
        in_specs=[SMEM] * small + [in_spec] * (len(arrays) - small - loose) + [ANY] * loose,
        out_specs=[out_spec] * len(outs),
        scratch_shapes=list(scratch),
        compiler_params=pltpu.CompilerParams(vmem_limit_bytes=12 * MIB),
        cost_estimate=pl.CostEstimate(flops=1, bytes_accessed=1, transcendentals=0),
    )(*arrays)


def after(value, *events):
    return lax.optimization_barrier((value, *events))[0]


def per_device(picture_embeds, caption_embeds, sharpness_factor, offset_term):
    scalars = (sharpness_factor, offset_term)
    n = lax.axis_size(AXES)
    rows, width = picture_embeds.shape
    one, two, square = (rows, width), (2 * rows, width), (rows, rows)
    here = lax.axis_index(AXES)
    rim = jnp.where(here == 0, 1, jnp.where(here == n - 1, 2, 0)).astype(jnp.int32).reshape(1)

    near = [(g, (g + 2) % n if g % 2 else (g - 2) % n) for g in range(n)]
    far = [(g, (g - 2) % n if g % 2 else (g + 2) % n) for g in range(n) if g not in (1, n - 2)]
    swap = [(g, g ^ 1) for g in range(n)]
    closing = [(0, n - 1), (n - 2, 0)]

    def sent(value, perm):
        return lax.ppermute(value, AXES, perm)

    mate_y = sent(caption_embeds, swap)
    (pair,) = call(
        prepare_kernel,
        [(two, BF16)],
        (picture_embeds, caption_embeds),
        in_spec=ANY,
        scratch=[pltpu.VMEM(two, BF16), pltpu.SemaphoreType.DMA((2 * CHUNKS,))],
    )
    near_pair = sent(pair, near)
    far_pair = sent(pair, far)
    mate_x = sent(picture_embeds, swap)
    picked, *mate_terms = call(
        early_kernel, [(two, BF16)] * 2 + [(square, BF16)] * 3, (rim, *scalars, pair, mate_x, mate_y), small=3
    )
    late_pair = sent(picked, closing)
    relayed_pair = sent(near_pair, swap)
    sums = call(
        middle_kernel,
        [(one, F32)] * 2,
        (*scalars, pair, *mate_terms, near_pair),
        small=2,
        loose=1,
        scratch=[pltpu.VMEM(two, BF16), pltpu.SemaphoreType.DMA(())],
    )
    return call(
        end_kernel,
        [(one, F32)] * 2,
        (rim, *scalars, pair, *sums, far_pair, relayed_pair, picture_embeds, caption_embeds, late_pair),
        small=3,
        loose=3,
        out_spec=ANY,
        scratch=[
            pltpu.VMEM(two, F32),
            pltpu.VMEM(two, BF16),
            pltpu.VMEM(two, BF16),
            pltpu.SemaphoreType.DMA((2,)),
            pltpu.SemaphoreType.DMA(()),
            pltpu.SemaphoreType.DMA((2 * CHUNKS,)),
        ],
    )


def solution(mesh):
    return jax.shard_map(
        per_device,
        mesh=mesh,
        in_specs=(P(AXES, None), P(AXES, None), P(), P()),
        out_specs=(P(AXES, None), P(AXES, None)),
        check_vma=False,
    )
```

profile of v0, /device:TPU:1, one launch (start us, length us, event | category | flops | bytes accessed | tf_op | source)
XLA Modules:
  0.0 52.1 jit_solution(632017841976148358)
XLA Ops:
  0.6 2.0 %shard_map.59.pair = bf16[512,1152]{1,0:T(8,128)(2,1)S(1)} custom-call(bf16[256,1152]{1,0:T(8,128)(2,1)} %x.3, bf16[256,1152]{1,0:T(8,128)(2,1)} %y.3), custom_call_target="tpu_custom_call" | custom-call | flops 1 | bytes 1 | tf_op jit(solution)/shard_map/pallas_call | solution.py:167
  2.7 3.9 %collective-permute-start.2 = (bf16[512,1152]{1,0:T(8,128)(2,1)S(1)}, bf16[512,1152]{1,0:T(8,128)(2,1)S(1)}, u32[]{:S(2)}, u32[]{:S(2)}) collective-permute-start(bf16[512,1152]{1,0:T(8,128)(2,1)S(1)} %shard_map.59.pair), channel_id=1, source_target_pairs={{0,1022},{1,3},{2,0},{3,5},{4,2},{5,7},{6,4},{7,9},{8,6},{9,11},{1... | collective-permute-start | bytes 3538952 | tf_op jit(solution)/shard_map/ppermute | solution.py:196
  6.6 22.8 %collective-permute-start = (bf16[256,1152]{1,0:T(8,128)(2,1)}, bf16[256,1152]{1,0:T(8,128)(2,1)}, u32[]{:S(2)}, u32[]{:S(2)}) collective-permute-start(bf16[256,1152]{1,0:T(8,128)(2,1)} %x.3), channel_id=1, source_target_pairs={{0,1},{1,0},{2,3},{3,2},{4,5},{5,4},{6,7},{7,6},{8,9},{9,8},{10,11... | collective-permute-start | bytes 1769480 | tf_op jit(solution)/shard_map/ppermute | solution.py:196
  29.4 1.9 %collective-permute-start.1 = (bf16[256,1152]{1,0:T(8,128)(2,1)}, bf16[256,1152]{1,0:T(8,128)(2,1)}, u32[]{:S(2)}, u32[]{:S(2)}) collective-permute-start(bf16[256,1152]{1,0:T(8,128)(2,1)} %y.3), channel_id=1, source_target_pairs={{0,1},{1,0},{2,3},{3,2},{4,5},{5,4},{6,7},{7,6},{8,9},{9,8},{10,11... | collective-permute-start | bytes 1769480 | tf_op jit(solution)/shard_map/ppermute | solution.py:196
  31.3 1.3 %collective-permute-start.3 = (bf16[512,1152]{1,0:T(8,128)(2,1)S(1)}, bf16[512,1152]{1,0:T(8,128)(2,1)S(1)}, u32[]{:S(2)}, u32[]{:S(2)}) collective-permute-start(bf16[512,1152]{1,0:T(8,128)(2,1)S(1)} %shard_map.59.pair), channel_id=1, source_target_pairs={{0,2},{2,4},{3,1},{4,6},{5,3},{6,8},{7,5},{8,10},{9,7},{10,12},{11... | collective-permute-start | bytes 3538952 | tf_op jit(solution)/shard_map/ppermute | solution.py:196
  33.9 0.0 collective-permute-done.mate_x
  34.0 0.0 collective-permute-done.1.mate_y
  34.0 2.5 %shard_map.60 = (bf16[512,1152]{1,0:T(8,128)(2,1)S(1)}, bf16[512,1152]{1,0:T(8,128)(2,1)S(1)}, bf16[256,256]{1,0:T(8,128)(2,1)S(1)}, bf16[256,256]{1,0:T(8,128)(2,1)S(1)}, bf16[256,256]{1,0:T(8,128)(2,1)S(1)}) custom-call(s32[1]{0:T(128)} %bitcast.rim, f32[1]{0:T(128)S(6)} %copy.6.scale, f32[1]{0:T(128)S(6)} %copy.7.offset, ...), custom_call_target="tpu_custom_call" | custom-call | flops 1 | bytes 1 | tf_op jit(solution)/shard_map/pallas_call | solution.py:167
  36.5 0.7 %collective-permute-start.5 = (bf16[512,1152]{1,0:T(8,128)(2,1)S(1)}, bf16[512,1152]{1,0:T(8,128)(2,1)S(1)}, u32[]{:S(2)}, u32[]{:S(2)}) collective-permute-start(bf16[512,1152]{1,0:T(8,128)(2,1)S(1)} %get-tuple-element.15), channel_id=1, source_target_pairs={{0,1023},{1022,0}} | collective-permute-start | bytes 3538952 | tf_op jit(solution)/shard_map/ppermute | solution.py:196
  37.2 2.9 %collective-permute-done.2.near = bf16[512,1152]{1,0:T(8,128)(2,1)S(1)} collective-permute-done((bf16[512,1152]{1,0:T(8,128)(2,1)S(1)}, bf16[512,1152]{1,0:T(8,128)(2,1)S(1)}, u32[]{:S(2)}, u32[]{:S(2)}) %collective-permute-start.2) | collective-permute-done | bytes 1179680 | tf_op jit(solution)/shard_map/ppermute | solution.py:196
  40.1 3.0 %collective-permute-start.4 = (bf16[512,1152]{1,0:T(8,128)(2,1)S(1)}, bf16[512,1152]{1,0:T(8,128)(2,1)S(1)}, u32[]{:S(2)}, u32[]{:S(2)}) collective-permute-start(bf16[512,1152]{1,0:T(8,128)(2,1)S(1)} %collective-permute-done.2.near), channel_id=1, source_target_pairs={{0,1},{1,0},{2,3},{3,2},{4,5},{5,4},{6,7},{7,6},{8,9},{9,8},{10,11... | collective-permute-start | bytes 3538952 | tf_op jit(solution)/shard_map/ppermute | solution.py:196
  43.1 2.1 %shard_map.61 = (f32[256,1152]{1,0:T(8,128)S(1)}, f32[256,1152]{1,0:T(8,128)S(1)}) custom-call(f32[1]{0:T(128)S(6)} %copy.6.scale, f32[1]{0:T(128)S(6)} %copy.7.offset, bf16[512,1152]{1,0:T(8,128)(2,1)S(1)} %shard_map.59.pair, bf16[512,1152]{1,0:T(8,128)(2,1)S(1)} %get-tuple-element.9.mates, bf16[256,256]{1,0:T(8,128)(2,1)S(1)} %get-tuple-element.10.own_grad, ...), custom_call_target="tpu_custom_call" | custom-call | flops 1 | bytes 1 | tf_op jit(solution)/shard_map/pallas_call | solution.py:167
  45.2 3.4 %collective-permute-done.3.far = bf16[512,1152]{1,0:T(8,128)(2,1)S(1)} collective-permute-done((bf16[512,1152]{1,0:T(8,128)(2,1)S(1)}, bf16[512,1152]{1,0:T(8,128)(2,1)S(1)}, u32[]{:S(2)}, u32[]{:S(2)}) %collective-permute-start.3) | collective-permute-done | bytes 1179680 | tf_op jit(solution)/shard_map/ppermute | solution.py:196
  48.6 0.0 collective-permute-done.5.late
  48.6 0.0 collective-permute-done.4.relayed
  48.6 3.5 %shard_map.62 = (f32[256,1152]{1,0:T(8,128)}, f32[256,1152]{1,0:T(8,128)}) custom-call(s32[1]{0:T(128)} %bitcast.rim, f32[1]{0:T(128)S(6)} %copy.6.scale, f32[1]{0:T(128)S(6)} %copy.7.offset, bf16[512,1152]{1,0:T(8,128)(2,1)S(1)} %shard_map.59.pair, f32[256,1152]{1,0:T(8,128)S(1)} %get-tuple-element.13.total_x, f32[256,1152]{1,0:T(8,128)S(1)} %get-tuple-element.14.total_y, ...), custom_call_target="tpu_custom_call" | custom-call | flops 1 | bytes 1 | tf_op jit(solution)/shard_map/pallas_call | solution.py:167
Async XLA Ops:
  2.7 37.5 %collective-permute-start.2 = (bf16[512,1152]{1,0:T(8,128)(2,1)S(1)}, bf16[512,1152]{1,0:T(8,128)(2,1)S(1)}, u32[]{:S(2)}, u32[]{:S(2)}) collective-permute-start(bf16[512,1152]{1,0:T(8,128)(2,1)S(1)} %shard_map.59.pair), channel_id=1, source_target_pairs={{0,1022},{1,3},{2,0},{3,5},{4,2},{5,7},{6,4},{7,9},{8,6},{9,11},{1... | collective-permute-start | bytes 3538952 | tf_op jit(solution)/shard_map/ppermute | solution.py:196
  6.6 27.3 %collective-permute-start = (bf16[256,1152]{1,0:T(8,128)(2,1)}, bf16[256,1152]{1,0:T(8,128)(2,1)}, u32[]{:S(2)}, u32[]{:S(2)}) collective-permute-start(bf16[256,1152]{1,0:T(8,128)(2,1)} %x.3), channel_id=1, source_target_pairs={{0,1},{1,0},{2,3},{3,2},{4,5},{5,4},{6,7},{7,6},{8,9},{9,8},{10,11... | collective-permute-start | bytes 1769480 | tf_op jit(solution)/shard_map/ppermute | solution.py:196
  29.4 4.6 %collective-permute-start.1 = (bf16[256,1152]{1,0:T(8,128)(2,1)}, bf16[256,1152]{1,0:T(8,128)(2,1)}, u32[]{:S(2)}, u32[]{:S(2)}) collective-permute-start(bf16[256,1152]{1,0:T(8,128)(2,1)} %y.3), channel_id=1, source_target_pairs={{0,1},{1,0},{2,3},{3,2},{4,5},{5,4},{6,7},{7,6},{8,9},{9,8},{10,11... | collective-permute-start | bytes 1769480 | tf_op jit(solution)/shard_map/ppermute | solution.py:196
  31.3 17.2 %collective-permute-start.3 = (bf16[512,1152]{1,0:T(8,128)(2,1)S(1)}, bf16[512,1152]{1,0:T(8,128)(2,1)S(1)}, u32[]{:S(2)}, u32[]{:S(2)}) collective-permute-start(bf16[512,1152]{1,0:T(8,128)(2,1)S(1)} %shard_map.59.pair), channel_id=1, source_target_pairs={{0,2},{2,4},{3,1},{4,6},{5,3},{6,8},{7,5},{8,10},{9,7},{10,12},{11... | collective-permute-start | bytes 3538952 | tf_op jit(solution)/shard_map/ppermute | solution.py:196
  36.5 12.1 %collective-permute-start.5 = (bf16[512,1152]{1,0:T(8,128)(2,1)S(1)}, bf16[512,1152]{1,0:T(8,128)(2,1)S(1)}, u32[]{:S(2)}, u32[]{:S(2)}) collective-permute-start(bf16[512,1152]{1,0:T(8,128)(2,1)S(1)} %get-tuple-element.15), channel_id=1, source_target_pairs={{0,1023},{1022,0}} | collective-permute-start | bytes 3538952 | tf_op jit(solution)/shard_map/ppermute | solution.py:196
  40.1 8.5 %collective-permute-start.4 = (bf16[512,1152]{1,0:T(8,128)(2,1)S(1)}, bf16[512,1152]{1,0:T(8,128)(2,1)S(1)}, u32[]{:S(2)}, u32[]{:S(2)}) collective-permute-start(bf16[512,1152]{1,0:T(8,128)(2,1)S(1)} %collective-permute-done.2.near), channel_id=1, source_target_pairs={{0,1},{1,0},{2,3},{3,2},{4,5},{5,4},{6,7},{7,6},{8,9},{9,8},{10,11... | collective-permute-start | bytes 3538952 | tf_op jit(solution)/shard_map/ppermute | solution.py:196
where the time goes:
time: 52.4 us; the launch traced here: 52.1 us
  starting transfers between devices  33.7 us (64%)
  Pallas kernels  10.1 us (19%)
  waiting for transfers between devices  6.29 us (12%)
  between operations  2.03 us (4%)
    ppermute x6, starting transfers between devices, sent(): return lax.ppermute(value, AXES, perm)  33.7 us
    pallas_call x4, Pallas kernels, call(): pl.pallas_call(kernel, out_shape=[jax.ShapeDtypeStruct(*o) for o in outs]...  10.1 us
    ppermute x6, waiting for transfers between devices, sent(): return lax.ppermute(value, AXES, perm)  6.29 us
  transfers between devices with their start and end apart: 6, of which 2 were waited for; matrix products, arithmetic and copies ran while one was open for 0% of the time, Pallas kernels for 9%

commit v1 on v0

--- a/solution.py
+++ b/solution.py
@@ -66,19 +66,30 @@
         pair[part] = (wide * inverse_norm(wide)).astype(BF16)
 
 
-def early_kernel(rim, scale, offset, pair, mate_x, mate_y, picked, mates, own_grad, mate_grad_x, mate_grad_y):
+def pick_kernel(rim, pair, mate_x, mate_y, picked, held, sem):
+    rows = mate_x.shape[0]
+
+    @pl.when(rim[0] == 1)
+    def _():
+        copies = [
+            pltpu.make_async_copy(source, held.at[pl.ds(side * rows, rows)], sem.at[side])
+            for side, source in enumerate((mate_x, mate_y))
+        ]
+        for copy in copies:
+            copy.start()
+        for copy in copies:
+            copy.wait()
+        picked[...] = normalized(held[...])
+
+    @pl.when(rim[0] != 1)
+    def _():
+        picked[...] = pair[...]
+
+
+def early_kernel(scale, offset, pair, mate_x, mate_y, mates, own_grad, mate_grad_x, mate_grad_y):
     rows = mate_x.shape[0]
     mates[:rows] = normalized(mate_x[...])
     mates[rows:] = normalized(mate_y[...])
-
-    @pl.when(rim[0] == 1)
-    def _():
-        picked[...] = mates[...]
-
-    @pl.when(rim[0] != 1)
-    def _():
-        picked[...] = pair[...]
-
     mine = halves(pair)
     z = logits(scale, offset, *mine)
     rows = lax.broadcasted_iota(jnp.int32, z.shape, 0)
@@ -89,21 +100,36 @@
 
 
 def middle_kernel(
-    scale, offset, pair, mates, own_grad, mate_grad_x, mate_grad_y, near, sum_x, sum_y, held, sem
+    rim, scale, offset, pair, mates, own_grad, mate_grad_x, mate_grad_y, near, first_far, sum_x, sum_y,
+    held, spare, sem,
 ):
-    copy = pltpu.make_async_copy(near, held, sem)
-    copy.start()
+    near_copy = pltpu.make_async_copy(near, held, sem.at[0])
+    near_copy.start()
+    first_copy = pltpu.make_async_copy(first_far, spare, sem.at[1])
+
+    @pl.when(rim[0] == 3)
+    def _():
+        first_copy.start()
+
     mine = halves(pair)
     mate_x, mate_y = halves(mates)
     sum_x[...] = dot(own_grad[...], mine[1]) + dot(mate_grad_x[...], mate_y)
     sum_y[...] = lax.dot_general(
         own_grad[...], mine[0], (((0,), (0,)), ((), ())), preferred_element_type=F32
     ) + dot(mate_grad_y[...], mate_x)
-    copy.wait()
+    near_copy.wait()
     nears = halves(held)
     grad_x, grad_y = side_grads(scale, offset, mine, nears)
     sum_x[...] += dot(grad_x, nears[1])
     sum_y[...] += dot(grad_y, nears[0])
+
+    @pl.when(rim[0] == 3)
+    def _():
+        first_copy.wait()
+        firsts = halves(spare)
+        first_grads = side_grads(scale, offset, mine, firsts)
+        sum_x[...] += dot(first_grads[0], firsts[1])
+        sum_y[...] += dot(first_grads[1], firsts[0])
 
 
 def end_kernel(
@@ -127,7 +153,7 @@
             total[...] + dot(far_grads[side], fars[1 - side]) + dot(relay_grads[side], relays[1 - side])
         )
 
-    @pl.when(rim[0] > 0)
+    @pl.when((rim[0] == 1) | (rim[0] == 2))
     def _():
         copy = pltpu.make_async_copy(late, spare, spare_sem)
         copy.start()
@@ -185,10 +211,10 @@
     rows, width = picture_embeds.shape
     one, two, square = (rows, width), (2 * rows, width), (rows, rows)
     here = lax.axis_index(AXES)
-    rim = jnp.where(here == 0, 1, jnp.where(here == n - 1, 2, 0)).astype(jnp.int32).reshape(1)
+    rim = jnp.where(here == 0, 1, jnp.where(here == n - 1, 2, jnp.where(here == 1, 3, 0))).astype(jnp.int32).reshape(1)
 
     near = [(g, (g + 2) % n if g % 2 else (g - 2) % n) for g in range(n)]
-    far = [(g, (g - 2) % n if g % 2 else (g + 2) % n) for g in range(n) if g not in (1, n - 2)]
+    far = [(g, (g - 2) % n if g % 2 else (g + 2) % n) for g in range(n) if g not in (1, 3, n - 2)]
     swap = [(g, g ^ 1) for g in range(n)]
     closing = [(0, n - 1), (n - 2, 0)]
 
@@ -205,19 +231,28 @@
     )
     near_pair = sent(pair, near)
     far_pair = sent(pair, far)
+    first_far = sent(pair, [(3, 1)])
     mate_x = sent(picture_embeds, swap)
-    picked, *mate_terms = call(
-        early_kernel, [(two, BF16)] * 2 + [(square, BF16)] * 3, (rim, *scalars, pair, mate_x, mate_y), small=3
-    )
-    late_pair = sent(picked, closing)
-    relayed_pair = sent(near_pair, swap)
+    (picked,) = call(
+        pick_kernel,
+        [(two, BF16)],
+        (rim, pair, mate_x, mate_y),
+        small=1,
+        loose=2,
+        scratch=[pltpu.VMEM(two, BF16), pltpu.SemaphoreType.DMA((2,))],
+    )
+    late_pair = sent(after(picked, first_far), closing)
+    mate_terms = call(
+        early_kernel, [(two, BF16)] + [(square, BF16)] * 3, (*scalars, pair, mate_x, mate_y), small=2
+    )
+    relayed_pair = sent(after(near_pair, *mate_terms), swap)
     sums = call(
         middle_kernel,
         [(one, F32)] * 2,
-        (*scalars, pair, *mate_terms, near_pair),
-        small=2,
-        loose=1,
-        scratch=[pltpu.VMEM(two, BF16), pltpu.SemaphoreType.DMA(())],
+        (rim, *scalars, pair, *mate_terms, near_pair, first_far),
+        small=3,
+        loose=2,
+        scratch=[pltpu.VMEM(two, BF16), pltpu.VMEM(two, BF16), pltpu.SemaphoreType.DMA((2,))],
     )
     return call(
         end_kernel,

time: 52.4 us -> 52.5 us (level)
  waiting for transfers between devices: 6.29 us -> 5.02 us
  starting transfers between devices: 33.7 us -> 34.7 us
    ppermute x6 -> x7, waiting for transfers between devices: 6.29 us -> 5.02 us  [sent(): return lax.ppermute(value, AXES, perm)]
    ppermute x6 -> x7, starting transfers between devices: 33.7 us -> 34.7 us  [sent(): return lax.ppermute(value, AXES, perm)]
    pallas_call x4 -> x5, Pallas kernels: 10.1 us -> 10.4 us  [call(): pl.pallas_call(kernel, out_shape=[jax.ShapeDtypeStruct(*o) for o in outs]...]
  transfers between devices with their start and end apart: 6 -> 7, of which waited for: 2 -> 2; matrix products, arithmetic and copies ran while one was open for 0% -> 0% of each run, Pallas kernels for 9% -> 9%
where the time goes in v1:
time: 52.5 us; the launch traced here: 52.2 us
  starting transfers between devices  34.7 us (66%)
  Pallas kernels  10.4 us (20%)
  waiting for transfers between devices  5.02 us (10%)
  between operations  2.07 us (4%)
    ppermute x7, starting transfers between devices, sent(): return lax.ppermute(value, AXES, perm)  34.7 us
    pallas_call x5, Pallas kernels, call(): pl.pallas_call(kernel, out_shape=[jax.ShapeDtypeStruct(*o) for o in outs]...  10.4 us
    ppermute x7, waiting for transfers between devices, sent(): return lax.ppermute(value, AXES, perm)  5.02 us
  transfers between devices with their start and end apart: 7, of which 2 were waited for; matrix products, arithmetic and copies ran while one was open for 0% of the time, Pallas kernels for 9%

profile of v1, /device:TPU:1, one launch (start us, length us, event | category | flops | bytes accessed | tf_op | source)
XLA Modules:
  0.0 52.2 jit_solution(7453059423113469849)
XLA Ops:
  0.6 2.0 %shard_map.59.pair = bf16[512,1152]{1,0:T(8,128)(2,1)S(1)} custom-call(bf16[256,1152]{1,0:T(8,128)(2,1)} %x.3, bf16[256,1152]{1,0:T(8,128)(2,1)} %y.3), custom_call_target="tpu_custom_call" | custom-call | flops 1 | bytes 1 | tf_op jit(solution)/shard_map/pallas_call | solution.py:193
  2.7 1.3 %collective-permute-start.3 = (bf16[512,1152]{1,0:T(8,128)(2,1)S(1)}, bf16[512,1152]{1,0:T(8,128)(2,1)}, u32[]{:S(2)}, u32[]{:S(2)}) collective-permute-start(bf16[512,1152]{1,0:T(8,128)(2,1)S(1)} %shard_map.59.pair), channel_id=1, source_target_pairs={{3,1}} | collective-permute-start | bytes 3538952 | tf_op jit(solution)/shard_map/ppermute | solution.py:222
  4.0 5.0 %collective-permute-start.2 = (bf16[512,1152]{1,0:T(8,128)(2,1)S(1)}, bf16[512,1152]{1,0:T(8,128)(2,1)}, u32[]{:S(2)}, u32[]{:S(2)}) collective-permute-start(bf16[512,1152]{1,0:T(8,128)(2,1)S(1)} %shard_map.59.pair), channel_id=1, source_target_pairs={{0,1022},{1,3},{2,0},{3,5},{4,2},{5,7},{6,4},{7,9},{8,6},{9,11},{1... | collective-permute-start | bytes 3538952 | tf_op jit(solution)/shard_map/ppermute | solution.py:222
  9.0 22.1 %collective-permute-start = (bf16[256,1152]{1,0:T(8,128)(2,1)}, bf16[256,1152]{1,0:T(8,128)(2,1)S(1)}, u32[]{:S(2)}, u32[]{:S(2)}) collective-permute-start(bf16[256,1152]{1,0:T(8,128)(2,1)} %x.3), channel_id=1, source_target_pairs={{0,1},{1,0},{2,3},{3,2},{4,5},{5,4},{6,7},{7,6},{8,9},{9,8},{10,11... | collective-permute-start | bytes 1769480 | tf_op jit(solution)/shard_map/ppermute | solution.py:222
  31.1 1.9 %collective-permute-start.1 = (bf16[256,1152]{1,0:T(8,128)(2,1)}, bf16[256,1152]{1,0:T(8,128)(2,1)S(1)}, u32[]{:S(2)}, u32[]{:S(2)}) collective-permute-start(bf16[256,1152]{1,0:T(8,128)(2,1)} %y.3), channel_id=1, source_target_pairs={{0,1},{1,0},{2,3},{3,2},{4,5},{5,4},{6,7},{7,6},{8,9},{9,8},{10,11... | collective-permute-start | bytes 1769480 | tf_op jit(solution)/shard_map/ppermute | solution.py:222
  33.0 0.7 %collective-permute-start.4 = (bf16[512,1152]{1,0:T(8,128)(2,1)S(1)}, bf16[512,1152]{1,0:T(8,128)(2,1)S(1)}, u32[]{:S(2)}, u32[]{:S(2)}) collective-permute-start(bf16[512,1152]{1,0:T(8,128)(2,1)S(1)} %shard_map.59.pair), channel_id=1, source_target_pairs={{0,2},{2,4},{4,6},{5,3},{6,8},{7,5},{8,10},{9,7},{10,12},{11,9},{1... | collective-permute-start | bytes 3538952 | tf_op jit(solution)/shard_map/ppermute | solution.py:222
  35.1 0.0 collective-permute-done.mate_x
  35.1 0.1 collective-permute-done.1.mate_y
  35.2 0.1 shard_map.62
  35.3 0.9 %shard_map.60 = (bf16[512,1152]{1,0:T(8,128)(2,1)S(1)}, bf16[256,256]{1,0:T(8,128)(2,1)S(1)}, bf16[256,256]{1,0:T(8,128)(2,1)S(1)}, bf16[256,256]{1,0:T(8,128)(2,1)S(1)}) custom-call(f32[1]{0:T(128)S(6)} %copy.6.scale, f32[1]{0:T(128)S(6)} %copy.7.offset, bf16[512,1152]{1,0:T(8,128)(2,1)S(1)} %shard_map.59.pair, ...), custom_call_target="tpu_custom_call" | custom-call | flops 1 | bytes 1 | tf_op jit(solution)/shard_map/pallas_call | solution.py:193
  36.3 0.0 collective-permute-done.3.first_far
  36.3 0.7 %collective-permute-start.6 = (bf16[512,1152]{1,0:T(8,128)(2,1)S(1)}, bf16[512,1152]{1,0:T(8,128)(2,1)S(1)}, u32[]{:S(2)}, u32[]{:S(2)}) collective-permute-start(bf16[512,1152]{1,0:T(8,128)(2,1)S(1)} %shard_map.62), channel_id=1, source_target_pairs={{0,1023},{1022,0}} | collective-permute-start | bytes 3538952 | tf_op jit(solution)/shard_map/ppermute | solution.py:222
  37.0 4.9 %collective-permute-done.2.near = bf16[512,1152]{1,0:T(8,128)(2,1)} collective-permute-done((bf16[512,1152]{1,0:T(8,128)(2,1)S(1)}, bf16[512,1152]{1,0:T(8,128)(2,1)}, u32[]{:S(2)}, u32[]{:S(2)}) %collective-permute-start.2) | collective-permute-done | bytes 1179680 | tf_op jit(solution)/shard_map/ppermute | solution.py:222
  41.9 2.9 %collective-permute-start.5 = (bf16[512,1152]{1,0:T(8,128)(2,1)}, bf16[512,1152]{1,0:T(8,128)(2,1)S(1)}, u32[]{:S(2)}, u32[]{:S(2)}) collective-permute-start(bf16[512,1152]{1,0:T(8,128)(2,1)} %collective-permute-done.2.near), channel_id=1, source_target_pairs={{0,1},{1,0},{2,3},{3,2},{4,5},{5,4},{6,7},{7,6},{8,9},{9,8},{10,11... | collective-permute-start | bytes 3538952 | tf_op jit(solution)/shard_map/ppermute | solution.py:222
  44.8 3.9 %shard_map.61 = (f32[256,1152]{1,0:T(8,128)S(1)}, f32[256,1152]{1,0:T(8,128)S(1)}) custom-call(s32[1]{0:T(128)} %bitcast.rim, f32[1]{0:T(128)S(6)} %copy.6.scale, f32[1]{0:T(128)S(6)} %copy.7.offset, bf16[512,1152]{1,0:T(8,128)(2,1)S(1)} %shard_map.59.pair, bf16[512,1152]{1,0:T(8,128)(2,1)S(1)} %get-tuple-element.10.mates, ...), custom_call_target="tpu_custom_call" | custom-call | flops 1 | bytes 1 | tf_op jit(solution)/shard_map/pallas_call | solution.py:193
  48.7 0.0 collective-permute-done.4.far
  48.7 0.0 collective-permute-done.6.late
  48.7 0.0 collective-permute-done.5.relayed
  48.7 3.5 %shard_map.63 = (f32[256,1152]{1,0:T(8,128)}, f32[256,1152]{1,0:T(8,128)}) custom-call(s32[1]{0:T(128)} %bitcast.rim, f32[1]{0:T(128)S(6)} %copy.6.scale, f32[1]{0:T(128)S(6)} %copy.7.offset, bf16[512,1152]{1,0:T(8,128)(2,1)S(1)} %shard_map.59.pair, f32[256,1152]{1,0:T(8,128)S(1)} %get-tuple-element.14.total_x, f32[256,1152]{1,0:T(8,128)S(1)} %get-tuple-element.15.total_y, ...), custom_call_target="tpu_custom_call" | custom-call | flops 1 | bytes 1 | tf_op jit(solution)/shard_map/pallas_call | solution.py:193
Async XLA Ops:
  2.7 33.6 %collective-permute-start.3 = (bf16[512,1152]{1,0:T(8,128)(2,1)S(1)}, bf16[512,1152]{1,0:T(8,128)(2,1)}, u32[]{:S(2)}, u32[]{:S(2)}) collective-permute-start(bf16[512,1152]{1,0:T(8,128)(2,1)S(1)} %shard_map.59.pair), channel_id=1, source_target_pairs={{3,1}} | collective-permute-start | bytes 3538952 | tf_op jit(solution)/shard_map/ppermute | solution.py:222
  4.0 38.0 %collective-permute-start.2 = (bf16[512,1152]{1,0:T(8,128)(2,1)S(1)}, bf16[512,1152]{1,0:T(8,128)(2,1)}, u32[]{:S(2)}, u32[]{:S(2)}) collective-permute-start(bf16[512,1152]{1,0:T(8,128)(2,1)S(1)} %shard_map.59.pair), channel_id=1, source_target_pairs={{0,1022},{1,3},{2,0},{3,5},{4,2},{5,7},{6,4},{7,9},{8,6},{9,11},{1... | collective-permute-start | bytes 3538952 | tf_op jit(solution)/shard_map/ppermute | solution.py:222
  9.0 26.1 %collective-permute-start = (bf16[256,1152]{1,0:T(8,128)(2,1)}, bf16[256,1152]{1,0:T(8,128)(2,1)S(1)}, u32[]{:S(2)}, u32[]{:S(2)}) collective-permute-start(bf16[256,1152]{1,0:T(8,128)(2,1)} %x.3), channel_id=1, source_target_pairs={{0,1},{1,0},{2,3},{3,2},{4,5},{5,4},{6,7},{7,6},{8,9},{9,8},{10,11... | collective-permute-start | bytes 1769480 | tf_op jit(solution)/shard_map/ppermute | solution.py:222
  31.1 4.1 %collective-permute-start.1 = (bf16[256,1152]{1,0:T(8,128)(2,1)}, bf16[256,1152]{1,0:T(8,128)(2,1)S(1)}, u32[]{:S(2)}, u32[]{:S(2)}) collective-permute-start(bf16[256,1152]{1,0:T(8,128)(2,1)} %y.3), channel_id=1, source_target_pairs={{0,1},{1,0},{2,3},{3,2},{4,5},{5,4},{6,7},{7,6},{8,9},{9,8},{10,11... | collective-permute-start | bytes 1769480 | tf_op jit(solution)/shard_map/ppermute | solution.py:222
  33.0 15.7 %collective-permute-start.4 = (bf16[512,1152]{1,0:T(8,128)(2,1)S(1)}, bf16[512,1152]{1,0:T(8,128)(2,1)S(1)}, u32[]{:S(2)}, u32[]{:S(2)}) collective-permute-start(bf16[512,1152]{1,0:T(8,128)(2,1)S(1)} %shard_map.59.pair), channel_id=1, source_target_pairs={{0,2},{2,4},{4,6},{5,3},{6,8},{7,5},{8,10},{9,7},{10,12},{11,9},{1... | collective-permute-start | bytes 3538952 | tf_op jit(solution)/shard_map/ppermute | solution.py:222
  36.3 12.4 %collective-permute-start.6 = (bf16[512,1152]{1,0:T(8,128)(2,1)S(1)}, bf16[512,1152]{1,0:T(8,128)(2,1)S(1)}, u32[]{:S(2)}, u32[]{:S(2)}) collective-permute-start(bf16[512,1152]{1,0:T(8,128)(2,1)S(1)} %shard_map.62), channel_id=1, source_target_pairs={{0,1023},{1022,0}} | collective-permute-start | bytes 3538952 | tf_op jit(solution)/shard_map/ppermute | solution.py:222
  41.9 6.8 %collective-permute-start.5 = (bf16[512,1152]{1,0:T(8,128)(2,1)}, bf16[512,1152]{1,0:T(8,128)(2,1)S(1)}, u32[]{:S(2)}, u32[]{:S(2)}) collective-permute-start(bf16[512,1152]{1,0:T(8,128)(2,1)} %collective-permute-done.2.near), channel_id=1, source_target_pairs={{0,1},{1,0},{2,3},{3,2},{4,5},{5,4},{6,7},{7,6},{8,9},{9,8},{10,11... | collective-permute-start | bytes 3538952 | tf_op jit(solution)/shard_map/ppermute | solution.py:222

commit v2 on v0

--- a/solution.py
+++ b/solution.py
@@ -9,7 +9,8 @@
 SPAN = 2 * HALF + 1
 AXES = ("outer", "blk")
 MIB = 1024 * 1024
-CHUNKS = 4
+CHUNKS = 8
+COLUMNS = 256
 F32, BF16 = jnp.float32, jnp.bfloat16
 
 
@@ -24,6 +25,16 @@
 
 def dot(a, b):
     return jnp.dot(a, b, preferred_element_type=F32)
+
+
+def accumulate(out, at, base, terms):
+    for start in range(0, out.shape[1], COLUMNS):
+        cols = slice(start, min(start + COLUMNS, out.shape[1]))
+        total = None if base is None else base[:, cols]
+        for a, b in terms:
+            part = dot(a, b[:, cols])
+            total = part if total is None else total + part
+        out[at, cols] = total
 
 
 def logits(scale, offset, own_n, other_n):
@@ -88,22 +99,16 @@
     mate_grad_x[...], mate_grad_y[...] = side_grads(scale, offset, mine, halves(mates))
 
 
-def middle_kernel(
-    scale, offset, pair, mates, own_grad, mate_grad_x, mate_grad_y, near, sum_x, sum_y, held, sem
-):
-    copy = pltpu.make_async_copy(near, held, sem)
-    copy.start()
-    mine = halves(pair)
+def middle_kernel(scale, offset, pair, mates, own_grad, mate_grad_x, mate_grad_y, near, sum_x, sum_y):
+    mine, nears = halves(pair), halves(near)
     mate_x, mate_y = halves(mates)
-    sum_x[...] = dot(own_grad[...], mine[1]) + dot(mate_grad_x[...], mate_y)
-    sum_y[...] = lax.dot_general(
-        own_grad[...], mine[0], (((0,), (0,)), ((), ())), preferred_element_type=F32
-    ) + dot(mate_grad_y[...], mate_x)
-    copy.wait()
-    nears = halves(held)
     grad_x, grad_y = side_grads(scale, offset, mine, nears)
-    sum_x[...] += dot(grad_x, nears[1])
-    sum_y[...] += dot(grad_y, nears[0])
+    accumulate(
+        sum_x, slice(None), None, [(own_grad[...], mine[1]), (mate_grad_x[...], mate_y), (grad_x, nears[1])]
+    )
+    accumulate(
+        sum_y, slice(None), None, [(own_grad[...].T, mine[0]), (mate_grad_y[...], mate_x), (grad_y, nears[0])]
+    )
 
 
 def end_kernel(
@@ -123,8 +128,11 @@
     far_grads = side_grads(scale, offset, mine, fars)
     relay_grads = side_grads(scale, offset, mine, relays)
     for side, total in enumerate((total_x, total_y)):
-        full[side * rows : (side + 1) * rows] = (
-            total[...] + dot(far_grads[side], fars[1 - side]) + dot(relay_grads[side], relays[1 - side])
+        accumulate(
+            full,
+            slice(side * rows, (side + 1) * rows),
+            total,
+            [(far_grads[side], fars[1 - side]), (relay_grads[side], relays[1 - side])],
         )
 
     @pl.when(rim[0] > 0)
@@ -216,8 +224,6 @@
         [(one, F32)] * 2,
         (*scalars, pair, *mate_terms, near_pair),
         small=2,
-        loose=1,
-        scratch=[pltpu.VMEM(two, BF16), pltpu.SemaphoreType.DMA(())],
     )
     return call(
         end_kernel,

time: 52.4 us -> 53.3 us (1.017)
  transfers between devices with their start and end apart: 6 -> 6, of which waited for: 2 -> 2; matrix products, arithmetic and copies ran while one was open for 0% -> 0% of each run, Pallas kernels for 9% -> 8%
where the time goes in v2:
time: 53.3 us; the launch traced here: 53 us
  starting transfers between devices  33.7 us (63%)
  Pallas kernels  10.5 us (20%)
  waiting for transfers between devices  6.8 us (13%)
  between operations  2.02 us (4%)
    ppermute x6, starting transfers between devices, sent(): return lax.ppermute(value, AXES, perm)  33.7 us
    pallas_call x4, Pallas kernels, call(): pl.pallas_call(kernel, out_shape=[jax.ShapeDtypeStruct(*o) for o in outs]...  10.5 us
    ppermute x6, waiting for transfers between devices, sent(): return lax.ppermute(value, AXES, perm)  6.8 us
  transfers between devices with their start and end apart: 6, of which 2 were waited for; matrix products, arithmetic and copies ran while one was open for 0% of the time, Pallas kernels for 8%

profile of v2, /device:TPU:1, one launch (start us, length us, event | category | flops | bytes accessed | tf_op | source)
XLA Modules:
  0.0 53.0 jit_solution(10908632354218424315)
XLA Ops:
  0.6 2.9 %shard_map.59.pair = bf16[512,1152]{1,0:T(8,128)(2,1)S(1)} custom-call(bf16[256,1152]{1,0:T(8,128)(2,1)} %x.3, bf16[256,1152]{1,0:T(8,128)(2,1)} %y.3), custom_call_target="tpu_custom_call" | custom-call | flops 1 | bytes 1 | tf_op jit(solution)/shard_map/pallas_call | solution.py:175
  3.5 3.9 %collective-permute-start.2 = (bf16[512,1152]{1,0:T(8,128)(2,1)S(1)}, bf16[512,1152]{1,0:T(8,128)(2,1)S(1)}, u32[]{:S(2)}, u32[]{:S(2)}) collective-permute-start(bf16[512,1152]{1,0:T(8,128)(2,1)S(1)} %shard_map.59.pair), channel_id=1, source_target_pairs={{0,1022},{1,3},{2,0},{3,5},{4,2},{5,7},{6,4},{7,9},{8,6},{9,11},{1... | collective-permute-start | bytes 3538952 | tf_op jit(solution)/shard_map/ppermute | solution.py:204
  7.5 22.8 %collective-permute-start = (bf16[256,1152]{1,0:T(8,128)(2,1)}, bf16[256,1152]{1,0:T(8,128)(2,1)}, u32[]{:S(2)}, u32[]{:S(2)}) collective-permute-start(bf16[256,1152]{1,0:T(8,128)(2,1)} %x.3), channel_id=1, source_target_pairs={{0,1},{1,0},{2,3},{3,2},{4,5},{5,4},{6,7},{7,6},{8,9},{9,8},{10,11... | collective-permute-start | bytes 1769480 | tf_op jit(solution)/shard_map/ppermute | solution.py:204
  30.3 1.9 %collective-permute-start.1 = (bf16[256,1152]{1,0:T(8,128)(2,1)}, bf16[256,1152]{1,0:T(8,128)(2,1)}, u32[]{:S(2)}, u32[]{:S(2)}) collective-permute-start(bf16[256,1152]{1,0:T(8,128)(2,1)} %y.3), channel_id=1, source_target_pairs={{0,1},{1,0},{2,3},{3,2},{4,5},{5,4},{6,7},{7,6},{8,9},{9,8},{10,11... | collective-permute-start | bytes 1769480 | tf_op jit(solution)/shard_map/ppermute | solution.py:204
  32.2 1.3 %collective-permute-start.3 = (bf16[512,1152]{1,0:T(8,128)(2,1)S(1)}, bf16[512,1152]{1,0:T(8,128)(2,1)S(1)}, u32[]{:S(2)}, u32[]{:S(2)}) collective-permute-start(bf16[512,1152]{1,0:T(8,128)(2,1)S(1)} %shard_map.59.pair), channel_id=1, source_target_pairs={{0,2},{2,4},{3,1},{4,6},{5,3},{6,8},{7,5},{8,10},{9,7},{10,12},{11... | collective-permute-start | bytes 3538952 | tf_op jit(solution)/shard_map/ppermute | solution.py:204
  34.8 0.0 collective-permute-done.mate_x
  34.8 0.0 collective-permute-done.1.mate_y
  34.8 2.5 %shard_map.60 = (bf16[512,1152]{1,0:T(8,128)(2,1)S(1)}, bf16[512,1152]{1,0:T(8,128)(2,1)S(1)}, bf16[256,256]{1,0:T(8,128)(2,1)S(1)}, bf16[256,256]{1,0:T(8,128)(2,1)S(1)}, bf16[256,256]{1,0:T(8,128)(2,1)S(1)}) custom-call(s32[1]{0:T(128)} %bitcast.rim, f32[1]{0:T(128)S(6)} %copy.6.scale, f32[1]{0:T(128)S(6)} %copy.7.offset, ...), custom_call_target="tpu_custom_call" | custom-call | flops 1 | bytes 1 | tf_op jit(solution)/shard_map/pallas_call | solution.py:175
  37.4 0.7 %collective-permute-start.5 = (bf16[512,1152]{1,0:T(8,128)(2,1)S(1)}, bf16[512,1152]{1,0:T(8,128)(2,1)S(1)}, u32[]{:S(2)}, u32[]{:S(2)}) collective-permute-start(bf16[512,1152]{1,0:T(8,128)(2,1)S(1)} %get-tuple-element.15), channel_id=1, source_target_pairs={{0,1023},{1022,0}} | collective-permute-start | bytes 3538952 | tf_op jit(solution)/shard_map/ppermute | solution.py:204
  38.1 2.9 %collective-permute-done.2.near = bf16[512,1152]{1,0:T(8,128)(2,1)S(1)} collective-permute-done((bf16[512,1152]{1,0:T(8,128)(2,1)S(1)}, bf16[512,1152]{1,0:T(8,128)(2,1)S(1)}, u32[]{:S(2)}, u32[]{:S(2)}) %collective-permute-start.2) | collective-permute-done | bytes 1179680 | tf_op jit(solution)/shard_map/ppermute | solution.py:204
  41.0 3.0 %collective-permute-start.4 = (bf16[512,1152]{1,0:T(8,128)(2,1)S(1)}, bf16[512,1152]{1,0:T(8,128)(2,1)S(1)}, u32[]{:S(2)}, u32[]{:S(2)}) collective-permute-start(bf16[512,1152]{1,0:T(8,128)(2,1)S(1)} %collective-permute-done.2.near), channel_id=1, source_target_pairs={{0,1},{1,0},{2,3},{3,2},{4,5},{5,4},{6,7},{7,6},{8,9},{9,8},{10,11... | collective-permute-start | bytes 3538952 | tf_op jit(solution)/shard_map/ppermute | solution.py:204
  44.0 1.6 %shard_map.61 = (f32[256,1152]{1,0:T(8,128)S(1)}, f32[256,1152]{1,0:T(8,128)S(1)}) custom-call(f32[1]{0:T(128)S(6)} %copy.6.scale, f32[1]{0:T(128)S(6)} %copy.7.offset, bf16[512,1152]{1,0:T(8,128)(2,1)S(1)} %shard_map.59.pair, bf16[512,1152]{1,0:T(8,128)(2,1)S(1)} %get-tuple-element.9.mates, bf16[256,256]{1,0:T(8,128)(2,1)S(1)} %get-tuple-element.10.own_grad, ...), custom_call_target="tpu_custom_call" | custom-call | flops 1 | bytes 1 | tf_op jit(solution)/shard_map/pallas_call | solution.py:175
  45.5 3.9 %collective-permute-done.3.far = bf16[512,1152]{1,0:T(8,128)(2,1)S(1)} collective-permute-done((bf16[512,1152]{1,0:T(8,128)(2,1)S(1)}, bf16[512,1152]{1,0:T(8,128)(2,1)S(1)}, u32[]{:S(2)}, u32[]{:S(2)}) %collective-permute-start.3) | collective-permute-done | bytes 1179680 | tf_op jit(solution)/shard_map/ppermute | solution.py:204
  49.4 0.0 collective-permute-done.5.late
  49.5 0.0 collective-permute-done.4.relayed
  49.5 3.5 %shard_map.62 = (f32[256,1152]{1,0:T(8,128)}, f32[256,1152]{1,0:T(8,128)}) custom-call(s32[1]{0:T(128)} %bitcast.rim, f32[1]{0:T(128)S(6)} %copy.6.scale, f32[1]{0:T(128)S(6)} %copy.7.offset, bf16[512,1152]{1,0:T(8,128)(2,1)S(1)} %shard_map.59.pair, f32[256,1152]{1,0:T(8,128)S(1)} %get-tuple-element.13.total_x, f32[256,1152]{1,0:T(8,128)S(1)} %get-tuple-element.14.total_y, ...), custom_call_target="tpu_custom_call" | custom-call | flops 1 | bytes 1 | tf_op jit(solution)/shard_map/pallas_call | solution.py:175
Async XLA Ops:
  3.5 37.5 %collective-permute-start.2 = (bf16[512,1152]{1,0:T(8,128)(2,1)S(1)}, bf16[512,1152]{1,0:T(8,128)(2,1)S(1)}, u32[]{:S(2)}, u32[]{:S(2)}) collective-permute-start(bf16[512,1152]{1,0:T(8,128)(2,1)S(1)} %shard_map.59.pair), channel_id=1, source_target_pairs={{0,1022},{1,3},{2,0},{3,5},{4,2},{5,7},{6,4},{7,9},{8,6},{9,11},{1... | collective-permute-start | bytes 3538952 | tf_op jit(solution)/shard_map/ppermute | solution.py:204
  7.5 27.3 %collective-permute-start = (bf16[256,1152]{1,0:T(8,128)(2,1)}, bf16[256,1152]{1,0:T(8,128)(2,1)}, u32[]{:S(2)}, u32[]{:S(2)}) collective-permute-start(bf16[256,1152]{1,0:T(8,128)(2,1)} %x.3), channel_id=1, source_target_pairs={{0,1},{1,0},{2,3},{3,2},{4,5},{5,4},{6,7},{7,6},{8,9},{9,8},{10,11... | collective-permute-start | bytes 1769480 | tf_op jit(solution)/shard_map/ppermute | solution.py:204
  30.3 4.6 %collective-permute-start.1 = (bf16[256,1152]{1,0:T(8,128)(2,1)}, bf16[256,1152]{1,0:T(8,128)(2,1)}, u32[]{:S(2)}, u32[]{:S(2)}) collective-permute-start(bf16[256,1152]{1,0:T(8,128)(2,1)} %y.3), channel_id=1, source_target_pairs={{0,1},{1,0},{2,3},{3,2},{4,5},{5,4},{6,7},{7,6},{8,9},{9,8},{10,11... | collective-permute-start | bytes 1769480 | tf_op jit(solution)/shard_map/ppermute | solution.py:204
  32.2 17.2 %collective-permute-start.3 = (bf16[512,1152]{1,0:T(8,128)(2,1)S(1)}, bf16[512,1152]{1,0:T(8,128)(2,1)S(1)}, u32[]{:S(2)}, u32[]{:S(2)}) collective-permute-start(bf16[512,1152]{1,0:T(8,128)(2,1)S(1)} %shard_map.59.pair), channel_id=1, source_target_pairs={{0,2},{2,4},{3,1},{4,6},{5,3},{6,8},{7,5},{8,10},{9,7},{10,12},{11... | collective-permute-start | bytes 3538952 | tf_op jit(solution)/shard_map/ppermute | solution.py:204
  37.4 12.1 %collective-permute-start.5 = (bf16[512,1152]{1,0:T(8,128)(2,1)S(1)}, bf16[512,1152]{1,0:T(8,128)(2,1)S(1)}, u32[]{:S(2)}, u32[]{:S(2)}) collective-permute-start(bf16[512,1152]{1,0:T(8,128)(2,1)S(1)} %get-tuple-element.15), channel_id=1, source_target_pairs={{0,1023},{1022,0}} | collective-permute-start | bytes 3538952 | tf_op jit(solution)/shard_map/ppermute | solution.py:204
  41.0 8.5 %collective-permute-start.4 = (bf16[512,1152]{1,0:T(8,128)(2,1)S(1)}, bf16[512,1152]{1,0:T(8,128)(2,1)S(1)}, u32[]{:S(2)}, u32[]{:S(2)}) collective-permute-start(bf16[512,1152]{1,0:T(8,128)(2,1)S(1)} %collective-permute-done.2.near), channel_id=1, source_target_pairs={{0,1},{1,0},{2,3},{3,2},{4,5},{5,4},{6,7},{7,6},{8,9},{9,8},{10,11... | collective-permute-start | bytes 3538952 | tf_op jit(solution)/shard_map/ppermute | solution.py:204
